TPU v7x, 128 devices: a whole 4x4x4 slice. The times are simulated.
128 devices in a mesh: gx: 16 (over x, y), gy: 8 (over z, core).
Axes of the slice: x: 4, y: 4, z: 4, core: 2. Of those that a mesh axis runs over, the one named last changes fastest.
Arguments:
- tokens: bfloat16 [16384, 2048], P(('gx', 'gy')), may hold values from -6 to 6
- out_grad: bfloat16 [16384, 2048], P(('gx', 'gy')), may hold values from -1.5 to 1.5
- expert_ids: int32 [16384, 8], P(('gx', 'gy')), may hold values from 0 to 127, all different within a row; in each aligned block of 128 rows (0 to 127, 128 to 255, ...) at most 9 rows name the same one
- gate_weights: bfloat16 [16384, 8], P(('gx', 'gy')), may hold values from 0.029907227 to 0.29882812
- w_gate: bfloat16 [128, 2048, 768], P(('gx', 'gy')), may hold values from -0.125 to 0.125
- w_up: bfloat16 [128, 2048, 768], P(('gx', 'gy')), may hold values from -0.125 to 0.125
- w_down: bfloat16 [128, 768, 2048], P(('gx', 'gy')), may hold values from -0.21875 to 0.21875
Outputs:
- token_grad: bfloat16 [16384, 2048], P(('gx', 'gy'))
- gate_grad: bfloat16 [16384, 8], P(('gx', 'gy'))
- grad_w_gate: bfloat16 [128, 2048, 768], P(('gx', 'gy'))
- grad_w_up: bfloat16 [128, 2048, 768], P(('gx', 'gy'))
- grad_w_down: bfloat16 [128, 768, 2048], P(('gx', 'gy'))
Inputs may be any that keep to these rules, and one draw needn't show every extreme that they name: `expert_ids`: each token names 8 different experts; among the 128 tokens of one device (an aligned block of rows) no expert is named more than 9 times, a bound that some block reaches.
All inputs are finite; a program needn't handle non-finite values.
Results may differ from a plain program's by a relative error of at most 0.011.
Values may be sent and summed in bfloat16 or wider, within the bound.
A program may use at most 128 MiB of HBM per device.

v0:
```python
import functools

import jax
import jax.numpy as jnp
from jax import lax
from jax.experimental import pallas as pl
from jax.experimental.pallas import tpu as pltpu
from jax.sharding import PartitionSpec as P

BF = jnp.bfloat16
F32 = jnp.float32
PEERS = 128
CAP = 9
GROUPS = 4
PER = PEERS // GROUPS
ROWS = PER * CAP
TILES = 16
MESH = pl.DeviceIdType.MESH
RIGHT = (((1,), (1,)), ((), ()))
CONTRACT = (((0,), (0,)), ((), ()))


def place(step, gx, gy, sign):
    i, j, k, c = step % 4, (step // 4) % 4, (step // 16) % 4, step // 64
    dx = (2 * i + 3 * j + k + 2 * c) % 4
    dy = (3 * i + c) % 4
    dz = (2 * i + 3 * k + 2 * c) % 4
    if sign < 0:
        dx, dy, dz = 4 - dx, 4 - dy, 4 - dz
    x, y, z, core = gx // 4, gx % 4, gy // 2, gy % 2
    return ((x + dx) % 4) * 4 + (y + dy) % 4, ((z + dz) % 4) * 2 + (core + c) % 2


def kernel(
    slot_tok, slot_gate, pair_slot, pair_pos, pair_rank, gates, tok, og, wg_h, wu_h, wd_h,
    tg, gg, gwg_h, gwu_h, gwd_h,
    sbuf, rbuf, x2, s2, act, gp, gu, wg, wu, wd, back, flat, gsend, gback,
    local_sem, w_sem, out_sem, ssem, rsem, bssem, brsem, gssem, grsem,
):
    gx, gy = lax.axis_index("gx"), lax.axis_index("gy")
    to = functools.partial(place, gx=gx, gy=gy)
    barrier = pltpu.get_barrier_semaphore()

    def greet(p, _):
        pl.semaphore_signal(barrier, inc=1, device_id=to(p, sign=1), device_id_type=MESH)
        return 0

    lax.fori_loop(1, PEERS, greet, 0)
    loads = [pltpu.make_async_copy(h, v, w_sem.at[i]) for i, (h, v) in enumerate(((wg_h, wg), (wu_h, wu), (wd_h, wd)))]
    for load in loads:
        load.start()

    def gather(p, _):
        for s in range(CAP):
            t = slot_tok[p * CAP + s]
            sbuf[p, 0, s] = tok[t]
            sbuf[p, 1, s] = (og[t].astype(F32) * slot_gate[p * CAP + s]).astype(BF)
        return 0

    lax.fori_loop(0, PEERS, gather, 0)
    pl.semaphore_wait(barrier, PEERS - 1)
    own = pltpu.make_async_copy(sbuf.at[0], rbuf.at[0], local_sem.at[0])
    own.start()

    def send(p, _):
        for half in range(2):
            pltpu.make_async_remote_copy(
                sbuf.at[p, half], rbuf.at[p, half], ssem.at[p // PER], rsem.at[p // PER],
                device_id=to(p, sign=1), device_id_type=MESH,
            ).start()
        return 0

    lax.fori_loop(1, PEERS, send, 0)
    for load in loads:
        load.wait()
    own.wait()

    def span(buf, g):
        return buf.at[pl.ds(1, PER - 1)] if g == 0 else buf.at[pl.ds(g * PER, PER)]

    def rows_span(buf, g):
        return buf.at[pl.ds(CAP, ROWS - CAP)] if g == 0 else buf.at[pl.ds(g * ROWS, ROWS)]

    def whole(src, dst, a, b):
        return pltpu.make_async_remote_copy(src, dst, a, b, device_id=to(1, sign=1), device_id_type=MESH)

    lane = lax.broadcasted_iota(jnp.int32, (ROWS, 128), 1)
    row = lax.broadcasted_iota(jnp.int32, (ROWS, 128), 0)
    own_lane = lane == row % CAP
    sel = lax.broadcasted_iota(jnp.int32, (PER, ROWS), 0) == lax.broadcasted_iota(jnp.int32, (PER, ROWS), 1) // CAP
    sel = sel.astype(F32).astype(BF)

    for g in range(GROUPS):
        whole(span(sbuf, g), span(rbuf, g), ssem.at[g], rsem.at[g]).wait()
        here = pl.ds(g * ROWS, ROWS)
        for half, dst in ((0, x2), (1, s2)):

            def spread(c, _, half=half):
                part = rbuf[g * PER + c, half].reshape(CAP * TILES, 128).astype(F32)
                flat[pl.ds(pl.multiple_of(c * CAP * TILES, CAP * TILES), CAP * TILES), :] = part
                return 0

            lax.fori_loop(0, PER, spread, 0)
            for j in range(TILES):
                dst[here, j * 128 : (j + 1) * 128] = flat[pl.ds(j, ROWS, stride=TILES), :].astype(BF)

        def hidden(c, total):
            cols = pl.ds(pl.multiple_of(c * 256, 256), 256)
            pre_gate = jnp.dot(x2[here, :], wg[:, cols], preferred_element_type=F32)
            pre_up = jnp.dot(x2[here, :], wu[:, cols], preferred_element_type=F32)
            sback = lax.dot_general(s2[here, :], wd[cols, :], RIGHT, preferred_element_type=F32)
            sigma = jax.nn.sigmoid(pre_gate)
            silu = pre_gate * sigma
            a = (silu * pre_up).astype(BF)
            act[here, cols] = a
            gu[here, cols] = (sback * silu).astype(BF)
            gp[here, cols] = (sback * pre_up * sigma * (1.0 + pre_gate * (1.0 - sigma))).astype(BF)
            return total + jnp.sum(sback * a.astype(F32), axis=1, keepdims=True)

        total = lax.fori_loop(0, 3, hidden, jnp.zeros((ROWS, 1), F32))
        spread_gate = jnp.where(own_lane, total, 0.0).astype(BF)
        gate_rows = jnp.dot(sel, spread_gate, preferred_element_type=F32)
        for c in range(PER):
            gsend[g * PER + c] = gate_rows[c : c + 1, :]

        def inputs(n, _):
            rows = pl.ds(pl.multiple_of(n * 256, 256), 256)
            part = lax.dot_general(gp[here, :], wg[rows, :], RIGHT, preferred_element_type=F32)
            part += lax.dot_general(gu[here, :], wu[rows, :], RIGHT, preferred_element_type=F32)
            flat[pl.ds(2 * n, ROWS, stride=TILES), :] = part[:, :128]
            flat[pl.ds(2 * n + 1, ROWS, stride=TILES), :] = part[:, 128:]
            return 0

        lax.fori_loop(0, 8, inputs, 0)

        def pack(c, _):
            part = flat[pl.ds(pl.multiple_of(c * CAP * TILES, CAP * TILES), CAP * TILES), :]
            sbuf[g * PER + c, 0] = part.astype(BF).reshape(CAP, TILES, 128)
            return 0

        lax.fori_loop(0, PER, pack, 0)

        def give(p, _):
            device = to(p, sign=-1)
            pltpu.make_async_remote_copy(
                sbuf.at[p, 0], back.at[pl.ds(p * CAP, CAP)], bssem.at[g], brsem.at[g],
                device_id=device, device_id_type=MESH,
            ).start()
            pltpu.make_async_remote_copy(
                gsend.at[p], gback.at[p], gssem.at[g], grsem.at[g], device_id=device, device_id_type=MESH
            ).start()
            return 0

        if g == 0:
            own_back = pltpu.make_async_copy(sbuf.at[0, 0], back.at[pl.ds(0, CAP)], local_sem.at[0])
            own_gate = pltpu.make_async_copy(gsend.at[0], gback.at[0], local_sem.at[1])
            own_back.start()
            own_gate.start()
        lax.fori_loop(max(1, g * PER), (g + 1) * PER, give, 0)

    def w_in(n, _):
        rows = pl.ds(pl.multiple_of(n * 256, 256), 256)
        xt = x2[:, rows]
        wg[rows, :] = lax.dot_general(xt, gp[...], CONTRACT, preferred_element_type=F32).astype(BF)
        wu[rows, :] = lax.dot_general(xt, gu[...], CONTRACT, preferred_element_type=F32).astype(BF)
        return 0

    def w_out(n, _):
        rows = pl.ds(pl.multiple_of((n // 2) * 256, 256), 256)
        cols = pl.ds(pl.multiple_of((n % 2) * 1024, 1024), 1024)
        wd[rows, cols] = lax.dot_general(act[:, rows], s2[:, cols], CONTRACT, preferred_element_type=F32).astype(BF)
        return 0

    stores = [pltpu.make_async_copy(v, h, out_sem.at[i]) for i, (h, v) in enumerate(((gwg_h, wg), (gwu_h, wu), (gwd_h, wd)))]
    lax.fori_loop(0, 8, w_in, 0)
    stores[0].start()
    stores[1].start()
    lax.fori_loop(0, 6, w_out, 0)
    stores[2].start()

    own_back.wait()
    own_gate.wait()
    for g in range(GROUPS):
        first = 1 if g == 0 else 0
        src = sbuf.at[pl.ds(g * PER + first, PER - first), 0]
        whole(src, rows_span(back, g), bssem.at[g], brsem.at[g]).wait()
        whole(span(gsend, g), span(gback, g), gssem.at[g], grsem.at[g]).wait()

    def combine(t, _):
        total = back[pair_slot[t * 8]].astype(F32)
        for k in range(1, 8):
            total += back[pair_slot[t * 8 + k]].astype(F32)
        tg[t] = total.astype(BF)
        return 0

    lax.fori_loop(0, 128, combine, 0)
    table = gback[...].reshape(PEERS, 128).astype(BF)
    lanes = lax.broadcasted_iota(jnp.int32, (128, 128), 1)
    lane8 = lax.broadcasted_iota(jnp.int32, (128, 8), 1)
    result = jnp.zeros((128, 8), F32)
    for k in range(8):
        pick = (lanes == pair_pos[:, k : k + 1]).astype(F32).astype(BF)
        found = jnp.dot(pick, table, preferred_element_type=F32)
        value = jnp.sum(jnp.where(lanes == pair_rank[:, k : k + 1], found, 0.0), axis=1, keepdims=True)
        result = jnp.where(lane8 == k, value, result)
    gg[...] = (result / gates[...].astype(F32)).astype(BF)
    for store in stores:
        store.wait()


def on_device(tokens, out_grad, expert_ids, gate_weights, w_gate, w_up, w_down):
    gx, gy = lax.axis_index("gx"), lax.axis_index("gy")
    tok, top = expert_ids.shape
    width, ff = w_gate.shape[1:]
    steps = jnp.arange(PEERS, dtype=jnp.int32)
    px, py = place(steps, gx, gy, 1)
    named = (expert_ids[:, :, None] == (px * 8 + py)).astype(F32)
    member = jnp.sum(named, axis=1)
    gate_of = jnp.sum(named * gate_weights.astype(F32)[:, :, None], axis=1)
    earlier = (jnp.arange(tok)[:, None] > jnp.arange(tok)[None, :]).astype(BF)
    rank = jnp.dot(earlier, member.astype(BF), preferred_element_type=F32)
    pair_pos = jnp.sum(named * steps.astype(F32), axis=2).astype(jnp.int32)
    pair_rank = jnp.sum(named * rank[:, None, :], axis=2).astype(jnp.int32)
    pair_slot = (pair_pos * CAP + pair_rank).reshape(tok * top)
    at = jnp.where(member > 0, rank, -1.0).T
    pick = (at[:, None, :] == jnp.arange(CAP, dtype=F32)[None, :, None]).astype(F32)
    slot_tok = jnp.sum(pick * jnp.arange(tok, dtype=F32), axis=2).astype(jnp.int32)
    slot_gate = jnp.sum(pick * gate_of.T[:, None, :], axis=2)

    smem, vmem, hbm = (pl.BlockSpec(memory_space=m) for m in (pltpu.SMEM, pltpu.VMEM, pl.ANY))
    dma = pltpu.SemaphoreType.DMA
    tg, gg, gwg, gwu, gwd = pl.pallas_call(
        kernel,
        out_shape=(
            jax.ShapeDtypeStruct((tok, TILES, 128), BF),
            jax.ShapeDtypeStruct((tok, top), BF),
            jax.ShapeDtypeStruct((width, ff), BF),
            jax.ShapeDtypeStruct((width, ff), BF),
            jax.ShapeDtypeStruct((ff, width), BF),
        ),
        in_specs=[smem] * 3 + [vmem] * 5 + [hbm] * 3,
        out_specs=(vmem, vmem, hbm, hbm, hbm),
        scratch_shapes=[
            pltpu.VMEM((PEERS, 2, CAP, TILES, 128), BF),
            pltpu.VMEM((PEERS, 2, CAP, TILES, 128), BF),
            pltpu.VMEM((PEERS * CAP, width), BF),
            pltpu.VMEM((PEERS * CAP, width), BF),
            pltpu.VMEM((PEERS * CAP, ff), BF),
            pltpu.VMEM((PEERS * CAP, ff), BF),
            pltpu.VMEM((PEERS * CAP, ff), BF),
            pltpu.VMEM((width, ff), BF),
            pltpu.VMEM((width, ff), BF),
            pltpu.VMEM((ff, width), BF),
            pltpu.VMEM((PEERS * CAP, TILES, 128), BF),
            pltpu.VMEM((ROWS * TILES, 128), F32),
            pltpu.VMEM((PEERS, 1, 128), F32),
            pltpu.VMEM((PEERS, 1, 128), F32),
            dma((2,)),
            dma((3,)),
            dma((3,)),
            dma((GROUPS,)),
            dma((GROUPS,)),
            dma((GROUPS,)),
            dma((GROUPS,)),
            dma((GROUPS,)),
            dma((GROUPS,)),
        ],
        compiler_params=pltpu.CompilerParams(collective_id=0, has_side_effects=True, vmem_limit_bytes=60 << 20),
        cost_estimate=pl.CostEstimate(flops=29 * 10**9, bytes_accessed=20 * 10**6, transcendentals=10**6),
        name="routed_backward",
    )(
        slot_tok.reshape(-1),
        slot_gate.reshape(-1),
        pair_slot,
        pair_pos,
        pair_rank,
        gate_weights,
        tokens.reshape(tok, TILES, 128),
        out_grad.reshape(tok, TILES, 128),
        w_gate[0],
        w_up[0],
        w_down[0],
    )
    return (tg.reshape(tok, width), gg, gwg[None], gwu[None], gwd[None])


def solution(mesh):
    both = ("gx", "gy")
    return jax.shard_map(
        on_device,
        mesh=mesh,
        in_specs=(P(both, None),) * 4 + (P(both, None, None),) * 3,
        out_specs=(P(both, None),) * 2 + (P(both, None, None),) * 3,
        check_vma=False,
    )
```

profile of v0, /device:TPU:1, one launch (start us, length us, event | category | flops | bytes accessed | tf_op | source)
XLA Modules:
  0.0 238.8 jit_solution(17088349832712442074)
XLA Ops:
  0.6 0.0 copy-start.2
  0.7 1.4 copy.28.gates
  2.1 0.8 copy.22
  2.9 0.2 fusion
  3.2 0.1 fusion.4
  3.3 0.1 copy.23
  3.4 0.8 copy.25
  4.2 0.6 fusion.2
  4.8 0.1 copy.26
  4.9 0.4 select_reduce_fusion
  5.3 0.1 copy.24
  5.4 0.8 convert_element_type.34.slot_tok
  6.2 0.1 copy.27
  6.3 0.8 reshape.198.slot_gate
  7.2 0.7 add.252.pair_slot
  7.8 0.6 convert_element_type.37.pair_pos
  8.5 0.6 convert_element_type.38.pair_rank
  9.1 1.9 copy.30
  11.1 0.0 copy-done.2
  11.1 0.9 copy.31
  12.0 214.8 %routed_backward.1 = (bf16[128,16,128]{2,1,0:T(8,128)(2,1)}, bf16[128,8]{1,0:T(8,128)(2,1)}, bf16[2048,768]{1,0:T(8,128)(2,1)}, bf16[2048,768]{1,0:T(8,128)(2,1)}, bf16[768,2048]{1,0:T(8,128)(2,1)}) custom-call(s32[1152]{0:T(1024)} %convert_element_type.34.slot_tok, f32[1152]{0:T(1024)} %reshape.198.slot_gate, s32[1024]{0:T(1024)} %add.252.pair_slot, ...), custom_call_target="tpu_custom_call" | custom-call | flops 28999999488 | bytes 20000000 | tf_op jit(solution)/shard_map/routed_backward/pallas_call | solution.py:232
  226.8 2.0 copy.34
  228.8 1.4 copy.29
  230.2 0.0 copy-start.1
  230.2 3.9 %copy.38 = bf16[1,2048,768]{2,1,0:T(8,128)(2,1)} copy(bf16[1,2048,768]{2,1,0:T(8,128)(2,1)} %bitcast.19) | data formatting | bytes 6291456
  234.1 0.0 copy-done.1
  234.1 0.0 copy-start
  234.1 1.7 copy.39
  235.8 1.4 copy-done
  237.1 1.7 copy.40
  (4 shorter events, 0.1 us)
Async XLA Ops:
  0.6 10.4 %copy-start.2 = (bf16[128,2048]{1,0:T(8,128)(2,1)S(1)}, bf16[128,2048]{1,0:T(8,128)(2,1)}, u32[]{:S(2)}) copy-start(bf16[128,2048]{1,0:T(8,128)(2,1)} %param.8) | copy-start | bytes 1572868
  230.2 3.9 %copy-start.1 = (bf16[2048,768]{1,0:T(8,128)(2,1)S(1)}, bf16[2048,768]{1,0:T(8,128)(2,1)}, u32[]{:S(2)}) copy-start(bf16[2048,768]{1,0:T(8,128)(2,1)} %get-tuple-element.13) | copy-start | bytes 9437188
  234.1 3.0 %copy-start = (bf16[768,2048]{1,0:T(8,128)(2,1)S(1)}, bf16[768,2048]{1,0:T(8,128)(2,1)}, u32[]{:S(2)}) copy-start(bf16[768,2048]{1,0:T(8,128)(2,1)} %get-tuple-element.14) | copy-start | bytes 9437188
where the time goes:
time: 239 us
  Pallas kernels  215 us (90%)
  local copies, waits for them, and re-layouts  20.5 us (9%)
  other arithmetic  2.56 us (1%)
    pallas_call x1, Pallas kernels, on_device(): pl.pallas_call(kernel, out_shape=(jax.ShapeDtypeStruct((tok, TILES, 128),...  215 us
    unnamed x15, local copies, waits for them, and re-layouts  17 us

commit v1 on v0

--- a/solution.py
+++ b/solution.py
@@ -21,20 +21,21 @@
 
 
 def place(step, gx, gy, sign):
-    i, j, k, c = step % 4, (step // 4) % 4, (step // 16) % 4, step // 64
-    dx = (2 * i + 3 * j + k + 2 * c) % 4
-    dy = (3 * i + c) % 4
-    dz = (2 * i + 3 * k + 2 * c) % 4
+    i, j, k, c = lax.rem(step, 4), lax.rem(lax.div(step, 4), 4), lax.rem(lax.div(step, 16), 4), lax.div(step, 64)
+    dx = 2 * i + 3 * j + k + 2 * c
+    dy = 3 * i + c
+    dz = 2 * i + 3 * k + 2 * c
+    x, y, z, core = lax.div(gx, 4), lax.rem(gx, 4), lax.div(gy, 2), lax.rem(gy, 2)
     if sign < 0:
-        dx, dy, dz = 4 - dx, 4 - dy, 4 - dz
-    x, y, z, core = gx // 4, gx % 4, gy // 2, gy % 2
-    return ((x + dx) % 4) * 4 + (y + dy) % 4, ((z + dz) % 4) * 2 + (core + c) % 2
+        dx, dy, dz = 32 - dx, 32 - dy, 32 - dz
+    return lax.rem(x + dx, 4) * 4 + lax.rem(y + dy, 4), lax.rem(z + dz, 4) * 2 + lax.rem(core + c, 2)
 
 
 def kernel(
-    slot_tok, slot_gate, pair_slot, pair_pos, pair_rank, gates, tok, og, wg_h, wu_h, wd_h,
+    ids, gates, tok, og, wg_h, wu_h, wd_h,
     tg, gg, gwg_h, gwu_h, gwd_h,
     sbuf, rbuf, x2, s2, act, gp, gu, wg, wu, wd, back, flat, gsend, gback,
+    tokt, ogt, ranks, tok_v, gate_v, pair_v, slot_tok, slot_gate, pair_slot, table_sem,
     local_sem, w_sem, out_sem, ssem, rsem, bssem, brsem, gssem, grsem,
 ):
     gx, gy = lax.axis_index("gx"), lax.axis_index("gy")
@@ -50,27 +51,82 @@
     for load in loads:
         load.start()
 
-    def gather(p, _):
+    step_of = lax.broadcasted_iota(jnp.int32, (PEERS, 128), 0)
+    tok_of = lax.broadcasted_iota(jnp.int32, (PEERS, 128), 1)
+    ex, ey = to(step_of, sign=1)
+    expert = ex * 8 + ey
+
+    def named(k):
+        return (expert == ids[k : k + 1, :]).astype(F32)
+
+    gate_rows8 = gates[...].astype(F32)
+    member = jnp.zeros((PEERS, 128), F32)
+    gate_of = jnp.zeros((PEERS, 128), F32)
+    for k in range(8):
+        member += named(k)
+        gate_of += named(k) * gate_rows8[k : k + 1, :]
+    earlier = (step_of < tok_of).astype(F32).astype(BF)
+    rank = jnp.dot(member.astype(BF), earlier, preferred_element_type=F32)
+    ranks[...] = rank
+    toks = jnp.zeros((PEERS, 128), F32)
+    slot_gates = jnp.zeros((PEERS, 128), F32)
+    tok_f = tok_of.astype(F32)
+    for s in range(CAP):
+        pick = jnp.where(rank == s, member, 0.0)
+        toks = jnp.where(tok_of == s, jnp.sum(pick * tok_f, axis=1, keepdims=True), toks)
+        slot_gates = jnp.where(tok_of == s, jnp.sum(pick * gate_of, axis=1, keepdims=True), slot_gates)
+    tok_v[...] = jnp.clip(toks.astype(jnp.int32), 0, 127)
+    gate_v[...] = slot_gates
+    slots = step_of.astype(F32) * CAP + rank
+    for k in range(8):
+        slot = jnp.sum(named(k) * slots, axis=0, keepdims=True).astype(jnp.int32)
+        pair_v[k : k + 1, :] = jnp.clip(slot, 0, PEERS * CAP - 1)
+    tables = [
+        pltpu.make_async_copy(v, m, table_sem.at[i])
+        for i, (v, m) in enumerate(((tok_v, slot_tok), (gate_v, slot_gate), (pair_v, pair_slot)))
+    ]
+    for table in tables:
+        table.start()
+    for src, dst in ((tok, tokt), (og, ogt)):
+        for j in range(TILES):
+            flat[pl.ds(j, 128, stride=TILES), :] = src[:, j * 128 : (j + 1) * 128].astype(F32)
+
+        def tile(c, _, dst=dst):
+            part = flat[pl.ds(pl.multiple_of(c * 8 * TILES, 8 * TILES), 8 * TILES), :]
+            dst[pl.ds(pl.multiple_of(c * 8, 8), 8)] = part.astype(BF).reshape(8, TILES, 128)
+            return 0
+
+        lax.fori_loop(0, 16, tile, 0)
+    for table in tables:
+        table.wait()
+
+    def gather_x(p, _):
         for s in range(CAP):
-            t = slot_tok[p * CAP + s]
-            sbuf[p, 0, s] = tok[t]
-            sbuf[p, 1, s] = (og[t].astype(F32) * slot_gate[p * CAP + s]).astype(BF)
-        return 0
-
-    lax.fori_loop(0, PEERS, gather, 0)
-    pl.semaphore_wait(barrier, PEERS - 1)
+            sbuf[p, 0, s] = tokt[slot_tok[p, s]]
+        return 0
+
+    def gather_dy(p, _):
+        for s in range(CAP):
+            sbuf[p, 1, s] = (ogt[slot_tok[p, s]].astype(F32) * slot_gate[p, s]).astype(BF)
+        return 0
+
+    def send(p, _, half, g):
+        pltpu.make_async_remote_copy(
+            sbuf.at[p, half], rbuf.at[p, half], ssem.at[g], rsem.at[g],
+            device_id=to(p, sign=1), device_id_type=MESH,
+        ).start()
+        return 0
+
+    for g in range(GROUPS):
+        lo, hi = g * PER, (g + 1) * PER
+        lax.fori_loop(lo, hi, gather_x, 0)
+        if g == 0:
+            pl.semaphore_wait(barrier, PEERS - 1)
+        lax.fori_loop(max(1, lo), hi, functools.partial(send, half=0, g=g), 0)
+        lax.fori_loop(lo, hi, gather_dy, 0)
+        lax.fori_loop(max(1, lo), hi, functools.partial(send, half=1, g=g), 0)
     own = pltpu.make_async_copy(sbuf.at[0], rbuf.at[0], local_sem.at[0])
     own.start()
-
-    def send(p, _):
-        for half in range(2):
-            pltpu.make_async_remote_copy(
-                sbuf.at[p, half], rbuf.at[p, half], ssem.at[p // PER], rsem.at[p // PER],
-                device_id=to(p, sign=1), device_id_type=MESH,
-            ).start()
-        return 0
-
-    lax.fori_loop(1, PEERS, send, 0)
     for load in loads:
         load.wait()
     own.wait()
@@ -187,58 +243,44 @@
         whole(span(gsend, g), span(gback, g), gssem.at[g], grsem.at[g]).wait()
 
     def combine(t, _):
-        total = back[pair_slot[t * 8]].astype(F32)
+        total = back[pair_slot[0, t]].astype(F32)
         for k in range(1, 8):
-            total += back[pair_slot[t * 8 + k]].astype(F32)
-        tg[t] = total.astype(BF)
+            total += back[pair_slot[k, t]].astype(F32)
+        flat[pl.ds(pl.multiple_of(t * TILES, TILES), TILES), :] = total
         return 0
 
     lax.fori_loop(0, 128, combine, 0)
-    table = gback[...].reshape(PEERS, 128).astype(BF)
-    lanes = lax.broadcasted_iota(jnp.int32, (128, 128), 1)
-    lane8 = lax.broadcasted_iota(jnp.int32, (128, 8), 1)
-    result = jnp.zeros((128, 8), F32)
+    for j in range(TILES):
+        tg[:, j * 128 : (j + 1) * 128] = flat[pl.ds(j, 128, stride=TILES), :].astype(BF)
+    table = gback[...].reshape(PEERS, 128)
+    rank = ranks[...]
+    found = jnp.zeros((PEERS, 128), F32)
+    for s in range(CAP):
+        found = jnp.where(rank == s, table[:, s : s + 1], found)
+    ex, ey = to(step_of, sign=1)
+    expert = ex * 8 + ey
     for k in range(8):
-        pick = (lanes == pair_pos[:, k : k + 1]).astype(F32).astype(BF)
-        found = jnp.dot(pick, table, preferred_element_type=F32)
-        value = jnp.sum(jnp.where(lanes == pair_rank[:, k : k + 1], found, 0.0), axis=1, keepdims=True)
-        result = jnp.where(lane8 == k, value, result)
-    gg[...] = (result / gates[...].astype(F32)).astype(BF)
+        value = jnp.sum((expert == ids[k : k + 1, :]).astype(F32) * found, axis=0, keepdims=True)
+        gg[k : k + 1, :] = (value / gates[k : k + 1, :].astype(F32)).astype(BF)
     for store in stores:
         store.wait()
 
 
 def on_device(tokens, out_grad, expert_ids, gate_weights, w_gate, w_up, w_down):
-    gx, gy = lax.axis_index("gx"), lax.axis_index("gy")
     tok, top = expert_ids.shape
     width, ff = w_gate.shape[1:]
-    steps = jnp.arange(PEERS, dtype=jnp.int32)
-    px, py = place(steps, gx, gy, 1)
-    named = (expert_ids[:, :, None] == (px * 8 + py)).astype(F32)
-    member = jnp.sum(named, axis=1)
-    gate_of = jnp.sum(named * gate_weights.astype(F32)[:, :, None], axis=1)
-    earlier = (jnp.arange(tok)[:, None] > jnp.arange(tok)[None, :]).astype(BF)
-    rank = jnp.dot(earlier, member.astype(BF), preferred_element_type=F32)
-    pair_pos = jnp.sum(named * steps.astype(F32), axis=2).astype(jnp.int32)
-    pair_rank = jnp.sum(named * rank[:, None, :], axis=2).astype(jnp.int32)
-    pair_slot = (pair_pos * CAP + pair_rank).reshape(tok * top)
-    at = jnp.where(member > 0, rank, -1.0).T
-    pick = (at[:, None, :] == jnp.arange(CAP, dtype=F32)[None, :, None]).astype(F32)
-    slot_tok = jnp.sum(pick * jnp.arange(tok, dtype=F32), axis=2).astype(jnp.int32)
-    slot_gate = jnp.sum(pick * gate_of.T[:, None, :], axis=2)
-
-    smem, vmem, hbm = (pl.BlockSpec(memory_space=m) for m in (pltpu.SMEM, pltpu.VMEM, pl.ANY))
+    vmem, hbm = pl.BlockSpec(memory_space=pltpu.VMEM), pl.BlockSpec(memory_space=pl.ANY)
     dma = pltpu.SemaphoreType.DMA
     tg, gg, gwg, gwu, gwd = pl.pallas_call(
         kernel,
         out_shape=(
-            jax.ShapeDtypeStruct((tok, TILES, 128), BF),
-            jax.ShapeDtypeStruct((tok, top), BF),
+            jax.ShapeDtypeStruct((tok, width), BF),
+            jax.ShapeDtypeStruct((top, tok), BF),
             jax.ShapeDtypeStruct((width, ff), BF),
             jax.ShapeDtypeStruct((width, ff), BF),
             jax.ShapeDtypeStruct((ff, width), BF),
         ),
-        in_specs=[smem] * 3 + [vmem] * 5 + [hbm] * 3,
+        in_specs=[vmem] * 4 + [hbm] * 3,
         out_specs=(vmem, vmem, hbm, hbm, hbm),
         scratch_shapes=[
             pltpu.VMEM((PEERS, 2, CAP, TILES, 128), BF),
@@ -255,6 +297,16 @@
             pltpu.VMEM((ROWS * TILES, 128), F32),
             pltpu.VMEM((PEERS, 1, 128), F32),
             pltpu.VMEM((PEERS, 1, 128), F32),
+            pltpu.VMEM((tok, TILES, 128), BF),
+            pltpu.VMEM((tok, TILES, 128), BF),
+            pltpu.VMEM((PEERS, tok), F32),
+            pltpu.VMEM((PEERS, 128), jnp.int32),
+            pltpu.VMEM((PEERS, 128), F32),
+            pltpu.VMEM((top, tok), jnp.int32),
+            pltpu.SMEM((PEERS, 128), jnp.int32),
+            pltpu.SMEM((PEERS, 128), F32),
+            pltpu.SMEM((top, tok), jnp.int32),
+            dma((3,)),
             dma((2,)),
             dma((3,)),
             dma((3,)),
@@ -269,19 +321,15 @@
         cost_estimate=pl.CostEstimate(flops=29 * 10**9, bytes_accessed=20 * 10**6, transcendentals=10**6),
         name="routed_backward",
     )(
-        slot_tok.reshape(-1),
-        slot_gate.reshape(-1),
-        pair_slot,
-        pair_pos,
-        pair_rank,
-        gate_weights,
-        tokens.reshape(tok, TILES, 128),
-        out_grad.reshape(tok, TILES, 128),
+        expert_ids.T,
+        gate_weights.T,
+        tokens,
+        out_grad,
         w_gate[0],
         w_up[0],
         w_down[0],
     )
-    return (tg.reshape(tok, width), gg, gwg[None], gwu[None], gwd[None])
+    return (tg, gg.T, gwg[None], gwu[None], gwd[None])
 
 
 def solution(mesh):

time: 239 us -> 216 us (0.904)
  the two profiles are of different devices: /device:TPU:1 before, /device:TPU:13 now
where the time goes in v1:
time: 216 us; the launch traced here: 215 us
  Pallas kernels  203 us (94%)
  local copies, waits for them, and re-layouts  11.7 us (5%)
    pallas_call x1, Pallas kernels, on_device(): pl.pallas_call(kernel, out_shape=(jax.ShapeDtypeStruct((tok, width), BF),...  203 us
    unnamed x9, local copies, waits for them, and re-layouts  11.7 us

profile of v1, /device:TPU:13, one launch (start us, length us, event | category | flops | bytes accessed | tf_op | source)
XLA Modules:
  0.0 215.4 jit_solution(6566195624056994743)
XLA Ops:
  0.6 203.0 %routed_backward.1 = (bf16[128,2048]{1,0:T(8,128)(2,1)}, bf16[8,128]{1,0:T(8,128)(2,1)}, bf16[2048,768]{1,0:T(8,128)(2,1)}, bf16[2048,768]{1,0:T(8,128)(2,1)}, bf16[768,2048]{1,0:T(8,128)(2,1)}) custom-call(s32[8,128]{1,0:T(8,128)} %bitcast.16, bf16[8,128]{1,0:T(8,128)(2,1)} %bitcast.17, bf16[128,2048]{1,0:T(8,128)(2,1)} %tok.1, bf16[128,2048]{1,0:T(8,128)(2,1)} %og.1, ...), custom_call_target="tpu_custom_call" | custom-call | flops 28999999488 | bytes 20000000 | tf_op jit(solution)/shard_map/routed_backward/pallas_call | solution.py:274
  203.6 1.9 copy.17
  205.5 1.2 copy.18
  206.8 0.0 copy-start.1
  206.8 3.9 %copy.19 = bf16[1,2048,768]{2,1,0:T(8,128)(2,1)} copy(bf16[1,2048,768]{2,1,0:T(8,128)(2,1)} %bitcast.11) | data formatting | bytes 6291456
  210.7 0.0 copy-done.1
  210.7 0.0 copy-start
  210.7 1.7 copy.20
  212.3 1.4 copy-done
  213.7 1.7 copy.21
Async XLA Ops:
  206.8 3.9 %copy-start.1 = (bf16[2048,768]{1,0:T(8,128)(2,1)S(1)}, bf16[2048,768]{1,0:T(8,128)(2,1)}, u32[]{:S(2)}) copy-start(bf16[2048,768]{1,0:T(8,128)(2,1)} %get-tuple-element.13) | copy-start | bytes 9437188
  210.7 3.0 %copy-start = (bf16[768,2048]{1,0:T(8,128)(2,1)S(1)}, bf16[768,2048]{1,0:T(8,128)(2,1)}, u32[]{:S(2)}) copy-start(bf16[768,2048]{1,0:T(8,128)(2,1)} %get-tuple-element.14) | copy-start | bytes 9437188

commit v2 on v1

--- a/solution.py
+++ b/solution.py
@@ -12,6 +12,8 @@
 PEERS = 128
 CAP = 9
 GROUPS = 4
+PARTS = 3
+PART = CAP // PARTS
 PER = PEERS // GROUPS
 ROWS = PER * CAP
 TILES = 16
@@ -29,6 +31,33 @@
     if sign < 0:
         dx, dy, dz = 32 - dx, 32 - dy, 32 - dz
     return lax.rem(x + dx, 4) * 4 + lax.rem(y + dy, 4), lax.rem(z + dz, 4) * 2 + lax.rem(core + c, 2)
+
+
+def each(g, gx, gy, sign, act):
+    x, y, z, core = lax.div(gx, 4), lax.rem(gx, 4), lax.div(gy, 2), lax.rem(gy, 2)
+    c = g // 2
+    other = lax.rem(core + c, 2)
+    ys = [lax.rem(y + (3 * i + c if sign > 0 else 16 - 3 * i - c), 4) for i in range(4)]
+
+    def serve(m, first):
+        j, k = lax.rem(m, 4), lax.div(m, 4) + 2 * (g % 2)
+        dx = 3 * j + k + 2 * c
+        dz = 3 * k + 2 * c
+        bx, bz = (x + dx, z + dz) if sign > 0 else (x + 32 - dx, z + 32 - dz)
+        even = lax.rem(bx, 4) * 4, lax.rem(bz, 4) * 2 + other
+        odd = lax.rem(bx + 2, 4) * 4, lax.rem(bz + 2, 4) * 2 + other
+        for i in range(first, 4):
+            a, b = odd if i % 2 else even
+            act(g * PER + m * 4 + i, (a + ys[i], b))
+
+    if g == 0:
+        serve(jnp.int32(0), 1)
+
+    def step(m, _):
+        serve(m, 0)
+        return 0
+
+    lax.fori_loop(1 if g == 0 else 0, PER // 4, step, 0)
 
 
 def kernel(
@@ -42,11 +71,11 @@
     to = functools.partial(place, gx=gx, gy=gy)
     barrier = pltpu.get_barrier_semaphore()
 
-    def greet(p, _):
-        pl.semaphore_signal(barrier, inc=1, device_id=to(p, sign=1), device_id_type=MESH)
-        return 0
-
-    lax.fori_loop(1, PEERS, greet, 0)
+    def greet(p, device):
+        pl.semaphore_signal(barrier, inc=1, device_id=device, device_id_type=MESH)
+
+    for g in range(GROUPS):
+        each(g, gx, gy, 1, greet)
     loads = [pltpu.make_async_copy(h, v, w_sem.at[i]) for i, (h, v) in enumerate(((wg_h, wg), (wu_h, wu), (wd_h, wd)))]
     for load in loads:
         load.start()
@@ -110,21 +139,23 @@
             sbuf[p, 1, s] = (ogt[slot_tok[p, s]].astype(F32) * slot_gate[p, s]).astype(BF)
         return 0
 
-    def send(p, _, half, g):
+    def send(p, device, half, g, part):
+        rows = pl.ds(part * PART, PART)
         pltpu.make_async_remote_copy(
-            sbuf.at[p, half], rbuf.at[p, half], ssem.at[g], rsem.at[g],
-            device_id=to(p, sign=1), device_id_type=MESH,
+            sbuf.at[p, half, rows], rbuf.at[p, half, rows], ssem.at[g], rsem.at[g],
+            device_id=device, device_id_type=MESH,
         ).start()
-        return 0
 
     for g in range(GROUPS):
         lo, hi = g * PER, (g + 1) * PER
         lax.fori_loop(lo, hi, gather_x, 0)
         if g == 0:
             pl.semaphore_wait(barrier, PEERS - 1)
-        lax.fori_loop(max(1, lo), hi, functools.partial(send, half=0, g=g), 0)
+        for part in range(PARTS):
+            each(g, gx, gy, 1, functools.partial(send, half=0, g=g, part=part))
         lax.fori_loop(lo, hi, gather_dy, 0)
-        lax.fori_loop(max(1, lo), hi, functools.partial(send, half=1, g=g), 0)
+        for part in range(PARTS):
+            each(g, gx, gy, 1, functools.partial(send, half=1, g=g, part=part))
     own = pltpu.make_async_copy(sbuf.at[0], rbuf.at[0], local_sem.at[0])
     own.start()
     for load in loads:
@@ -196,23 +227,25 @@
 
         lax.fori_loop(0, PER, pack, 0)
 
-        def give(p, _):
-            device = to(p, sign=-1)
+        def give(p, device, part):
             pltpu.make_async_remote_copy(
-                sbuf.at[p, 0], back.at[pl.ds(p * CAP, CAP)], bssem.at[g], brsem.at[g],
-                device_id=device, device_id_type=MESH,
+                sbuf.at[p, 0, pl.ds(part * PART, PART)], back.at[pl.ds(p * CAP + part * PART, PART)],
+                bssem.at[g], brsem.at[g], device_id=device, device_id_type=MESH,
             ).start()
+
+        def give_gate(p, device):
             pltpu.make_async_remote_copy(
                 gsend.at[p], gback.at[p], gssem.at[g], grsem.at[g], device_id=device, device_id_type=MESH
             ).start()
-            return 0
 
         if g == 0:
             own_back = pltpu.make_async_copy(sbuf.at[0, 0], back.at[pl.ds(0, CAP)], local_sem.at[0])
             own_gate = pltpu.make_async_copy(gsend.at[0], gback.at[0], local_sem.at[1])
             own_back.start()
             own_gate.start()
-        lax.fori_loop(max(1, g * PER), (g + 1) * PER, give, 0)
+        for part in range(PARTS):
+            each(g, gx, gy, -1, functools.partial(give, part=part))
+        each(g, gx, gy, -1, give_gate)
 
     def w_in(n, _):
         rows = pl.ds(pl.multiple_of(n * 256, 256), 256)

time: 216 us -> 187 us (0.87)
  the two profiles are of different devices: /device:TPU:13 before, /device:TPU:1 now
where the time goes in v2:
time: 187 us
  Pallas kernels  175 us (94%)
  local copies, waits for them, and re-layouts  11.7 us (6%)
    pallas_call x1, Pallas kernels, on_device(): pl.pallas_call(kernel, out_shape=(jax.ShapeDtypeStruct((tok, width), BF),...  175 us
    unnamed x9, local copies, waits for them, and re-layouts  11.7 us

profile of v2, /device:TPU:1, one launch (start us, length us, event | category | flops | bytes accessed | tf_op | source)
XLA Modules:
  0.0 187.0 jit_solution(4906833168698065335)
XLA Ops:
  0.6 174.6 %routed_backward.1 = (bf16[128,2048]{1,0:T(8,128)(2,1)}, bf16[8,128]{1,0:T(8,128)(2,1)}, bf16[2048,768]{1,0:T(8,128)(2,1)}, bf16[2048,768]{1,0:T(8,128)(2,1)}, bf16[768,2048]{1,0:T(8,128)(2,1)}) custom-call(s32[8,128]{1,0:T(8,128)} %bitcast.16, bf16[8,128]{1,0:T(8,128)(2,1)} %bitcast.17, bf16[128,2048]{1,0:T(8,128)(2,1)} %tok.1, bf16[128,2048]{1,0:T(8,128)(2,1)} %og.1, ...), custom_call_target="tpu_custom_call" | custom-call | flops 28999999488 | bytes 20000000 | tf_op jit(solution)/shard_map/routed_backward/pallas_call | solution.py:307
  175.3 1.9 %copy.17 = bf16[128,2048]{1,0:T(8,128)(2,1)} copy(bf16[128,2048]{1,0:T(8,128)(2,1)} %get-tuple-element.20) | data formatting | bytes 1048576
  177.1 1.2 copy.18
  178.4 0.0 copy-start.1
  178.4 3.9 %copy.19 = bf16[1,2048,768]{2,1,0:T(8,128)(2,1)} copy(bf16[1,2048,768]{2,1,0:T(8,128)(2,1)} %bitcast.11) | data formatting | bytes 6291456
  182.3 0.0 copy-done.1
  182.3 0.0 copy-start
  182.3 1.7 copy.20
  184.0 1.4 copy-done
  185.3 1.7 copy.21
Async XLA Ops:
  178.4 3.9 %copy-start.1 = (bf16[2048,768]{1,0:T(8,128)(2,1)S(1)}, bf16[2048,768]{1,0:T(8,128)(2,1)}, u32[]{:S(2)}) copy-start(bf16[2048,768]{1,0:T(8,128)(2,1)} %get-tuple-element.13) | copy-start | bytes 9437188
  182.3 3.0 %copy-start = (bf16[768,2048]{1,0:T(8,128)(2,1)S(1)}, bf16[768,2048]{1,0:T(8,128)(2,1)}, u32[]{:S(2)}) copy-start(bf16[768,2048]{1,0:T(8,128)(2,1)} %get-tuple-element.14) | copy-start | bytes 9437188

commit v3 on v2

--- a/solution.py
+++ b/solution.py
@@ -77,9 +77,6 @@
     for g in range(GROUPS):
         each(g, gx, gy, 1, greet)
     loads = [pltpu.make_async_copy(h, v, w_sem.at[i]) for i, (h, v) in enumerate(((wg_h, wg), (wu_h, wu), (wd_h, wd)))]
-    for load in loads:
-        load.start()
-
     step_of = lax.broadcasted_iota(jnp.int32, (PEERS, 128), 0)
     tok_of = lax.broadcasted_iota(jnp.int32, (PEERS, 128), 1)
     ex, ey = to(step_of, sign=1)
@@ -116,18 +113,19 @@
     ]
     for table in tables:
         table.start()
-    for src, dst in ((tok, tokt), (og, ogt)):
+    def to_tiles(src, dst):
         for j in range(TILES):
             flat[pl.ds(j, 128, stride=TILES), :] = src[:, j * 128 : (j + 1) * 128].astype(F32)
 
-        def tile(c, _, dst=dst):
+        def tile(c, _):
             part = flat[pl.ds(pl.multiple_of(c * 8 * TILES, 8 * TILES), 8 * TILES), :]
             dst[pl.ds(pl.multiple_of(c * 8, 8), 8)] = part.astype(BF).reshape(8, TILES, 128)
             return 0
 
         lax.fori_loop(0, 16, tile, 0)
-    for table in tables:
-        table.wait()
+
+    to_tiles(tok, tokt)
+    tables[0].wait()
 
     def gather_x(p, _):
         for s in range(CAP):
@@ -153,6 +151,12 @@
             pl.semaphore_wait(barrier, PEERS - 1)
         for part in range(PARTS):
             each(g, gx, gy, 1, functools.partial(send, half=0, g=g, part=part))
+        if g == 0:
+            to_tiles(og, ogt)
+            tables[1].wait()
+            tables[2].wait()
+            for load in loads:
+                load.start()
         lax.fori_loop(lo, hi, gather_dy, 0)
         for part in range(PARTS):
             each(g, gx, gy, 1, functools.partial(send, half=1, g=g, part=part))
@@ -243,9 +247,9 @@
             own_gate = pltpu.make_async_copy(gsend.at[0], gback.at[0], local_sem.at[1])
             own_back.start()
             own_gate.start()
+        each(g, gx, gy, -1, give_gate)
         for part in range(PARTS):
             each(g, gx, gy, -1, functools.partial(give, part=part))
-        each(g, gx, gy, -1, give_gate)
 
     def w_in(n, _):
         rows = pl.ds(pl.multiple_of(n * 256, 256), 256)
@@ -270,21 +274,7 @@
     own_back.wait()
     own_gate.wait()
     for g in range(GROUPS):
-        first = 1 if g == 0 else 0
-        src = sbuf.at[pl.ds(g * PER + first, PER - first), 0]
-        whole(src, rows_span(back, g), bssem.at[g], brsem.at[g]).wait()
         whole(span(gsend, g), span(gback, g), gssem.at[g], grsem.at[g]).wait()
-
-    def combine(t, _):
-        total = back[pair_slot[0, t]].astype(F32)
-        for k in range(1, 8):
-            total += back[pair_slot[k, t]].astype(F32)
-        flat[pl.ds(pl.multiple_of(t * TILES, TILES), TILES), :] = total
-        return 0
-
-    lax.fori_loop(0, 128, combine, 0)
-    for j in range(TILES):
-        tg[:, j * 128 : (j + 1) * 128] = flat[pl.ds(j, 128, stride=TILES), :].astype(BF)
     table = gback[...].reshape(PEERS, 128)
     rank = ranks[...]
     found = jnp.zeros((PEERS, 128), F32)
@@ -295,6 +285,21 @@
     for k in range(8):
         value = jnp.sum((expert == ids[k : k + 1, :]).astype(F32) * found, axis=0, keepdims=True)
         gg[k : k + 1, :] = (value / gates[k : k + 1, :].astype(F32)).astype(BF)
+    for g in range(GROUPS):
+        first = 1 if g == 0 else 0
+        src = sbuf.at[pl.ds(g * PER + first, PER - first), 0]
+        whole(src, rows_span(back, g), bssem.at[g], brsem.at[g]).wait()
+
+    def combine(t, _):
+        total = back[pair_slot[0, t]].astype(F32)
+        for k in range(1, 8):
+            total += back[pair_slot[k, t]].astype(F32)
+        flat[pl.ds(pl.multiple_of(t * TILES, TILES), TILES), :] = total
+        return 0
+
+    lax.fori_loop(0, 128, combine, 0)
+    for j in range(TILES):
+        tg[:, j * 128 : (j + 1) * 128] = flat[pl.ds(j, 128, stride=TILES), :].astype(BF)
     for store in stores:
         store.wait()
 

time: 187 us -> 185 us (0.989)
  Pallas kernels: 175 us -> 172 us
    pallas_call x1, Pallas kernels: 175 us -> 172 us  [on_device(): pl.pallas_call(kernel, out_shape=(jax.ShapeDtypeStruct((tok, width), BF),...]
where the time goes in v3:
time: 185 us; the launch traced here: 184 us
  Pallas kernels  172 us (93%)
  local copies, waits for them, and re-layouts  11.7 us (6%)
    pallas_call x1, Pallas kernels, on_device(): pl.pallas_call(kernel, out_shape=(jax.ShapeDtypeStruct((tok, width), BF),...  172 us
    unnamed x9, local copies, waits for them, and re-layouts  11.7 us

profile of v3, /device:TPU:1, one launch (start us, length us, event | category | flops | bytes accessed | tf_op | source)
XLA Modules:
  0.0 184.5 jit_solution(192982239553722890)
XLA Ops:
  0.6 172.1 %routed_backward.1 = (bf16[128,2048]{1,0:T(8,128)(2,1)}, bf16[8,128]{1,0:T(8,128)(2,1)}, bf16[2048,768]{1,0:T(8,128)(2,1)}, bf16[2048,768]{1,0:T(8,128)(2,1)}, bf16[768,2048]{1,0:T(8,128)(2,1)}) custom-call(s32[8,128]{1,0:T(8,128)} %bitcast.16, bf16[8,128]{1,0:T(8,128)(2,1)} %bitcast.17, bf16[128,2048]{1,0:T(8,128)(2,1)} %tok.1, bf16[128,2048]{1,0:T(8,128)(2,1)} %og.1, ...), custom_call_target="tpu_custom_call" | custom-call | flops 28999999488 | bytes 20000000 | tf_op jit(solution)/shard_map/routed_backward/pallas_call | solution.py:312
  172.7 1.9 %copy.17 = bf16[128,2048]{1,0:T(8,128)(2,1)} copy(bf16[128,2048]{1,0:T(8,128)(2,1)} %get-tuple-element.20) | data formatting | bytes 1048576
  174.6 1.2 copy.18
  175.9 0.0 copy-start.1
  175.9 3.9 %copy.19 = bf16[1,2048,768]{2,1,0:T(8,128)(2,1)} copy(bf16[1,2048,768]{2,1,0:T(8,128)(2,1)} %bitcast.11) | data formatting | bytes 6291456
  179.8 0.0 copy-done.1
  179.8 0.0 copy-start
  179.8 1.7 copy.20
  181.4 1.4 copy-done
  182.8 1.7 copy.21
Async XLA Ops:
  175.9 3.9 %copy-start.1 = (bf16[2048,768]{1,0:T(8,128)(2,1)S(1)}, bf16[2048,768]{1,0:T(8,128)(2,1)}, u32[]{:S(2)}) copy-start(bf16[2048,768]{1,0:T(8,128)(2,1)} %get-tuple-element.13) | copy-start | bytes 9437188
  179.8 3.0 %copy-start = (bf16[768,2048]{1,0:T(8,128)(2,1)S(1)}, bf16[768,2048]{1,0:T(8,128)(2,1)}, u32[]{:S(2)}) copy-start(bf16[768,2048]{1,0:T(8,128)(2,1)} %get-tuple-element.14) | copy-start | bytes 9437188
